TPU v7x, 32 devices: a whole 2x2x4 slice. The times are simulated.
32 devices in a mesh: seq: 8 (over y, x, core), head: 4 (over z).
Axes of the slice: x: 2, y: 2, z: 4, core: 2. Of those that a mesh axis runs over, the one named last changes fastest.
Arguments:
- queries: bfloat16 [3072, 1024], P('seq', 'head'), may hold values from -6 to 6
- key_rows: bfloat16 [3072, 1024], P('seq', 'head'), may hold values from -6 to 6
- value_rows: bfloat16 [3072, 1024], P('seq', 'head'), may hold values from -6 to 6
- out_weight: bfloat16 [4096, 1024], P(None, 'head'), may hold values from -0.1875 to 0.1875
- out_grad: bfloat16 [3072, 4096], P('seq'), may hold values from -6 to 6
Outputs:
- output: bfloat16 [3072, 4096], P(('seq', 'head'))
- query_grad: bfloat16 [3072, 1024], P('seq', 'head')
- key_grad: bfloat16 [3072, 1024], P('seq', 'head')
- value_grad: bfloat16 [3072, 1024], P('seq', 'head')
- weight_grad: float32 [4096, 1024], P('seq', 'head')
All inputs are finite; a program needn't handle non-finite values.
Results may differ from a plain program's by a relative error of at most 0.02.
Values may be sent and summed in bfloat16 or wider, within the bound.
A program may use at most 64 MiB of HBM per device.

v0:
```python
import jax
import jax.numpy as jnp
from jax import lax
from jax.sharding import PartitionSpec as P

HD = 128
CH = 64


def swapped(block, axis, distance):
    count = lax.axis_size(axis)
    route = []
    for low in range(count):
        high = low | 1 << distance
        if high != low and high < count:
            route += [(low, high), (high, low)]
    return lax.ppermute(block, axis, route)


def split_state(state):
    upper = state.astype(jnp.bfloat16)
    lower = (state - upper.astype(jnp.float32)).astype(jnp.bfloat16)
    return (upper, lower)


def state_product(form, operand, parts):
    first = jnp.einsum(form, operand, parts[0], preferred_element_type=jnp.float32)
    return first + jnp.einsum(form, operand, parts[1], preferred_element_type=jnp.float32)


def local(queries, key_rows, value_rows, out_weight, out_grad):
    local_rows = queries.shape[0]
    head_count = queries.shape[1] // HD
    blocks = local_rows // CH
    total_rows = local_rows * lax.axis_size("seq")
    factor = (HD * total_rows) ** (-0.5)
    block_shape = (blocks, CH, head_count, HD)
    flat_shape = (local_rows, head_count * HD)
    query_blocks = queries.reshape(block_shape)
    key_blocks = key_rows.reshape(block_shape)
    value_blocks = value_rows.reshape(block_shape)
    causal = (jnp.arange(CH)[:, None] >= jnp.arange(CH)[None, :])[None, None]
    grad_rows = jnp.dot(out_grad, out_weight, preferred_element_type=jnp.float32).astype(
        jnp.bfloat16
    )
    grad_blocks = grad_rows.reshape(block_shape)
    key_value = jnp.einsum(
        "cshd,cshe->chde", key_blocks, value_blocks, preferred_element_type=jnp.float32
    )
    query_pairs = jnp.einsum(
        "cthd,cthe->chde", query_blocks, grad_blocks, preferred_element_type=jnp.float32
    )
    own_state = jnp.sum(key_value, 0)
    own_pairs = jnp.sum(query_pairs, 0)
    empty_state = jnp.zeros_like(own_state)
    position = lax.axis_index("seq")
    level_count = lax.axis_size("seq").bit_length() - 1
    inflow = empty_state
    outflow = empty_state
    state_total = own_state
    pairs_total = own_pairs
    for level in range(level_count):
        other_state, other_pairs = (
            swapped(state_total.astype(jnp.bfloat16), "seq", level).astype(state_total.dtype),
            swapped(pairs_total.astype(jnp.bfloat16), "seq", level).astype(pairs_total.dtype),
        )
        upper_half = position >> level & 1 == 1
        inflow = inflow + jnp.where(upper_half, other_state, 0.0)
        outflow = outflow + jnp.where(upper_half, 0.0, other_pairs)
        state_total = state_total + other_state
        pairs_total = pairs_total + other_pairs
    before = inflow[None] + jnp.cumsum(key_value, 0) - key_value
    later_state = outflow[None] + own_pairs[None] - jnp.cumsum(query_pairs, 0)
    before_parts = split_state(before)
    later_parts = split_state(later_state)
    scores = jnp.einsum(
        "cthd,cshd->chts", query_blocks, key_blocks, preferred_element_type=jnp.float32
    )
    weights = jnp.where(causal, factor * scores, 0.0).astype(jnp.bfloat16)
    within = jnp.einsum(
        "chts,cshe->cthe", weights, value_blocks, preferred_element_type=jnp.float32
    )
    carried = factor * state_product("cthd,chde->cthe", query_blocks, before_parts)
    attention = (within + carried).astype(jnp.bfloat16).reshape(flat_shape)
    output = lax.psum_scatter(
        lax.dot_general(
            attention, out_weight, (((1,), (1,)), ((), ())), preferred_element_type=jnp.float32
        ).astype(jnp.bfloat16),
        "head",
        scatter_dimension=0,
        tiled=True,
    )
    grad_scores = jnp.einsum(
        "cthe,cshe->chts", grad_blocks, value_blocks, preferred_element_type=jnp.float32
    )
    grad_weights = jnp.where(causal, factor * grad_scores, 0.0).astype(jnp.bfloat16)
    query_grad = jnp.einsum(
        "chts,cshd->cthd", grad_weights, key_blocks, preferred_element_type=jnp.float32
    )
    query_grad = query_grad + factor * state_product("cthe,chde->cthd", grad_blocks, before_parts)
    key_grad = jnp.einsum(
        "chts,cthd->cshd", grad_weights, query_blocks, preferred_element_type=jnp.float32
    )
    key_grad = key_grad + factor * state_product("cshe,chde->cshd", value_blocks, later_parts)
    value_grad = jnp.einsum(
        "chts,cthe->cshe", weights, grad_blocks, preferred_element_type=jnp.float32
    )
    value_grad = value_grad + factor * state_product("cshd,chde->cshe", key_blocks, later_parts)
    weight_grad = lax.psum_scatter(
        lax.dot_general(
            out_grad, attention, (((0,), (0,)), ((), ())), preferred_element_type=jnp.float32
        ),
        "seq",
        scatter_dimension=0,
        tiled=True,
    ) * total_rows ** (-0.5)
    return (
        output,
        query_grad.astype(jnp.bfloat16).reshape(flat_shape),
        key_grad.astype(jnp.bfloat16).reshape(flat_shape),
        value_grad.astype(jnp.bfloat16).reshape(flat_shape),
        weight_grad,
    )


def solution(mesh):
    return jax.shard_map(
        local,
        mesh=mesh,
        in_specs=(
            P("seq", "head"),
            P("seq", "head"),
            P("seq", "head"),
            P(None, "head"),
            P("seq", None),
        ),
        out_specs=(
            P(("seq", "head"), None),
            P("seq", "head"),
            P("seq", "head"),
            P("seq", "head"),
            P("seq", "head"),
        ),
        check_vma=False,
    )
```

profile of v0, /device:TPU:11, one launch (start us, length us, event | category | flops | bytes accessed | tf_op | source)
XLA Modules:
  0.0 165.2 jit_solution(5604113565822837807)
XLA Ops:
  7.2 1.1 reshape.49
  9.2 3.3 %convolution_convert_fusion.1 = bf16[384,256]{1,0:T(8,128)(2,1)} fusion(bf16[384,4096]{1,0:T(8,128)(2,1)S(1)} %copy-done, bf16[4096,256]{1,0:T(8,128)(2,1)} %param.8), kind=kOutput, calls=%fused_computation.32 | convolution fusion | flops 805404672 | bytes 5439488 | tf_op jit(solution)/shard_map/dot_general | solution.py:43
  12.5 1.0 reshape.53
  13.5 1.9 %fusion.62 = (f32[2,128,128]{1,2,0:T(8,128)}, f32[6,2,128,128]{2,3,1,0:T(8,128)}) fusion(bf16[6,64,2,128]{3,2,1,0:T(2,128)(2,1)S(1)} %reshape.49, bf16[6,64,2,128]{3,2,1,0:T(2,128)(2,1)S(1)} %reshape.53), kind=kOutput, calls=%fused_computation.92 | convolution fusion | flops 25329664 | bytes 1310720 | tf_op jit(solution)/shard_map/cthd,cthe->chde/dot_general | solution.py:50
  15.4 1.0 copy.120
  17.7 1.0 reshape.50
  18.7 1.0 reshape.51
  20.9 0.9 fusion.63
  23.1 1.3 collective-permute-start.1
  24.4 2.2 %collective-permute-done.4 = bf16[2,128,128]{2,1,0:T(8,128)(2,1)S(1)} collective-permute-done((bf16[2,128,128]{2,1,0:T(8,128)(2,1)S(1)}, bf16[2,128,128]{2,1,0:T(8,128)(2,1)S(1)}, u32[]{:S(2)}, u32[]{:S(2)}) %collective-permute-start.4) | collective-permute-done | bytes 65568 | tf_op jit(solution)/shard_map/ppermute | solution.py:17
  26.6 1.5 fusion.30
  28.1 1.2 collective-permute-start.5
  31.5 2.4 %collective-permute-done.2 = bf16[2,128,128]{2,1,0:T(8,128)(2,1)} collective-permute-done((bf16[2,128,128]{2,1,0:T(8,128)(2,1)}, bf16[2,128,128]{2,1,0:T(8,128)(2,1)}, u32[]{:S(2)}, u32[]{:S(2)}) %collective-permute-start.2) | collective-permute-done | bytes 65568 | tf_op jit(solution)/shard_map/ppermute | solution.py:17
  33.9 1.8 %fusion.25 = (f32[2,128,128]{2,1,0:T(8,128)S(1)}, f32[2,128,128]{2,1,0:T(8,128)}) fusion(bf16[2,128,128]{2,1,0:T(8,128)(2,1)} %copy-done.18, bf16[2,128,128]{2,1,0:T(8,128)(2,1)} %copy-done.20, bf16[2,128,128]{2,1,0:T(8,128)(2,1)} %collective-permute-done.2, pred[]{:T(512)S(6)} %eq.11, pred[]{:T(512)S(6)} %eq.10, pred[]{:T(512)S(6)} %eq.9, ...), kind=kLoop, calls=%fused_computation.55 | loop fusion | flops 557056 | bytes 786435 | tf_op jit(solution)/shard_map/add | solution.py:68
  35.6 1.6 subtract_convert_fusion.1
  39.1 3.2 %convolution_bitcast_fusion = f32[4096,256]{0,1:T(8,128)} fusion(bf16[384,4096]{1,0:T(8,128)(2,1)S(1)} %copy-done, bf16[48,8,2,128]{3,2,1,0:T(2,128)(2,1)S(1)} %bitcast.66), kind=kOutput, calls=%fused_computation.1 | convolution fusion | flops 805306368 | bytes 7536640 | tf_op jit(solution)/shard_map/dot_general | solution.py:110
  42.4 4.4 %convolution_convert_fusion = bf16[384,4096]{1,0:T(8,128)(2,1)} fusion(bf16[4096,256]{1,0:T(8,128)(2,1)} %param.8, bf16[48,8,2,128]{3,2,1,0:T(2,128)(2,1)} %bitcast.67), kind=kOutput, calls=%fused_computation | convolution fusion | flops 806879232 | bytes 5439488 | tf_op jit(solution)/shard_map/dot_general | solution.py:86
  46.9 1.8 %fusion.12 = bf16[6,2,64,64]{3,2,1,0:T(8,128)(2,1)} fusion(pred[64,64]{1,0:T(8,128)(4,1)S(1)} %iota_compare_fusion, bf16[6,64,2,128]{3,2,1,0:T(2,128)(2,1)} %copy-done.2, bf16[6,64,2,128]{3,2,1,0:T(2,128)(2,1)S(1)} %reshape.51), kind=kOutput, calls=%fused_computation.26 | convolution fusion | flops 12730368 | bytes 495616 | tf_op jit(solution)/shard_map/cthe,cshe->chts/dot_general | solution.py:93
  48.7 1.6 copy.123
  50.4 1.3 reduce-window_subtract_fusion
  57.2 38.3 %reduce-scatter.5.cloned.1.call-done = f32[512,256]{0,1:T(8,128)} async-done(((f32[4096,256]{0,1:T(8,128)}), f32[512,256]{0,1:T(8,128)}) %reduce-scatter.5.cloned.1.call-update) | async-done | bytes 524304 | tf_op jit(solution)/shard_map/reduce_scatter | solution.py:109
  95.5 1.9 %broadcast_multiply_fusion = f32[512,256]{0,1:T(8,128)} fusion(f32[512,256]{0,1:T(8,128)} %reduce-scatter.5.cloned.1.call-done), kind=kLoop, calls=%fused_computation.37 | loop fusion | flops 131072 | bytes 1048576 | tf_op jit(solution)/shard_map/mul | solution.py:109
  97.3 2.0 %copy.136 = f32[512,256]{1,0:T(8,128)} copy(f32[512,256]{0,1:T(8,128)} %broadcast_multiply_fusion) | data formatting | bytes 1048576
  99.4 59.0 %reduce-scatter.3.cloned.1.call-done = bf16[96,4096]{1,0:T(8,128)(2,1)} async-done(((bf16[384,4096]{1,0:T(8,128)(2,1)}), bf16[96,4096]{1,0:T(8,128)(2,1)}) %reduce-scatter.3.cloned.1.call-update) | async-done | bytes 786448 | tf_op jit(solution)/shard_map/reduce_scatter | solution.py:85
  (81 shorter events, 14.1 us)
Async XLA Ops:
  7.2 2.0 %copy-start = (bf16[384,4096]{1,0:T(8,128)(2,1)S(1)}, bf16[384,4096]{1,0:T(8,128)(2,1)}, u32[]{:S(2)}) copy-start(bf16[384,4096]{1,0:T(8,128)(2,1)} %param.9) | copy-start | bytes 9437188
  7.2 88.3 %reduce-scatter.5.cloned.1.call-start = ((), (), s32[]{:S(2)}) async-start(), calls=%async_computation.3 | async-start | bytes 4718592 | tf_op jit(solution)/shard_map/reduce_scatter | solution.py:109
  9.2 4.3 %copy-start.4 = (bf16[6,64,2,128]{3,2,1,0:T(2,128)(2,1)}, bf16[6,64,2,128]{3,2,1,0:T(2,128)(2,1)S(1)}, u32[]{:S(2)}) copy-start(bf16[6,64,2,128]{3,2,1,0:T(2,128)(2,1)S(1)} %reshape.49) | copy-start | bytes 589828
  13.5 3.6 %copy-start.2 = (bf16[6,64,2,128]{3,2,1,0:T(2,128)(2,1)}, bf16[6,64,2,128]{3,2,1,0:T(2,128)(2,1)S(1)}, u32[]{:S(2)}) copy-start(bf16[6,64,2,128]{3,2,1,0:T(2,128)(2,1)S(1)} %reshape.53) | copy-start | bytes 589828
  17.1 4.8 %collective-permute-start.3 = (bf16[2,128,128]{2,1,0:T(8,128)(2,1)}, bf16[2,128,128]{2,1,0:T(8,128)(2,1)}, u32[]{:S(2)}, u32[]{:S(2)}) collective-permute-start(bf16[2,128,128]{2,1,0:T(8,128)(2,1)} %convert_element_type.96), channel_id=1, source_target_pairs={{0,4},{4,0},{8,12},{12,8},{16,20},{20,16},{24,28},{28,24},{1,5},{5... | collective-permute-start | bytes 196616 | tf_op jit(solution)/shard_map/ppermute | solution.py:17
  19.7 2.2 %copy-start.13 = (f32[2,128,128]{2,1,0:T(8,128)S(1)}, f32[2,128,128]{2,1,0:T(8,128)}, u32[]{:S(2)}) copy-start(f32[2,128,128]{2,1,0:T(8,128)} %copy-done.12) | copy-start | bytes 393220
  19.7 10.5 %copy-start.5 = (bf16[6,64,2,128]{3,2,1,0:T(2,128)(2,1)S(1)}, bf16[6,64,2,128]{3,2,1,0:T(2,128)(2,1)}, u32[]{:S(2)}) copy-start(bf16[6,64,2,128]{3,2,1,0:T(2,128)(2,1)} %copy-done.4) | copy-start | bytes 589828
  20.1 3.0 %collective-permute-start = (bf16[2,128,128]{2,1,0:T(8,128)(2,1)S(1)}, bf16[2,128,128]{2,1,0:T(8,128)(2,1)S(1)}, u32[]{:S(2)}, u32[]{:S(2)}) collective-permute-start(bf16[2,128,128]{2,1,0:T(8,128)(2,1)S(1)} %convert_element_type.82), channel_id=1, source_target_pairs={{0,4},{4,0},{8,12},{12,8},{16,20},{20,16},{24,28},{28,24},{1,5},{5... | collective-permute-start | bytes 196616 | tf_op jit(solution)/shard_map/ppermute | solution.py:17
  22.8 3.8 %collective-permute-start.4 = (bf16[2,128,128]{2,1,0:T(8,128)(2,1)S(1)}, bf16[2,128,128]{2,1,0:T(8,128)(2,1)S(1)}, u32[]{:S(2)}, u32[]{:S(2)}) collective-permute-start(bf16[2,128,128]{2,1,0:T(8,128)(2,1)S(1)} %fusion.57), channel_id=1, source_target_pairs={{0,8},{8,0},{4,12},{12,4},{16,24},{24,16},{20,28},{28,20},{1,9},{9... | collective-permute-start | bytes 196616 | tf_op jit(solution)/shard_map/ppermute | solution.py:17
  23.1 8.0 %copy-start.18 = (bf16[2,128,128]{2,1,0:T(8,128)(2,1)}, bf16[2,128,128]{2,1,0:T(8,128)(2,1)S(1)}, u32[]{:S(2)}) copy-start(bf16[2,128,128]{2,1,0:T(8,128)(2,1)S(1)} %collective-permute-done) | copy-start | bytes 196612
  23.1 6.2 %collective-permute-start.1 = (bf16[2,128,128]{2,1,0:T(8,128)(2,1)S(1)}, bf16[2,128,128]{2,1,0:T(8,128)(2,1)S(1)}, u32[]{:S(2)}, u32[]{:S(2)}) collective-permute-start(bf16[2,128,128]{2,1,0:T(8,128)(2,1)S(1)} %fusion.56), channel_id=1, source_target_pairs={{0,8},{8,0},{4,12},{12,4},{16,24},{24,16},{20,28},{28,20},{1,9},{9... | collective-permute-start | bytes 196616 | tf_op jit(solution)/shard_map/ppermute | solution.py:17
  26.6 4.6 %copy-start.19 = (bf16[2,128,128]{2,1,0:T(8,128)(2,1)}, bf16[2,128,128]{2,1,0:T(8,128)(2,1)S(1)}, u32[]{:S(2)}) copy-start(bf16[2,128,128]{2,1,0:T(8,128)(2,1)S(1)} %collective-permute-done.4) | copy-start | bytes 196612
  28.1 3.4 %collective-permute-start.5 = (bf16[2,128,128]{2,1,0:T(8,128)(2,1)}, bf16[2,128,128]{2,1,0:T(8,128)(2,1)}, u32[]{:S(2)}, u32[]{:S(2)}) collective-permute-start(bf16[2,128,128]{2,1,0:T(8,128)(2,1)} %fusion.30), channel_id=1, source_target_pairs={{0,16},{16,0},{4,20},{20,4},{8,24},{24,8},{12,28},{28,12},{1,17},{... | collective-permute-start | bytes 196616 | tf_op jit(solution)/shard_map/ppermute | solution.py:17
  29.3 1.8 %copy-start.20 = (bf16[2,128,128]{2,1,0:T(8,128)(2,1)}, bf16[2,128,128]{2,1,0:T(8,128)(2,1)S(1)}, u32[]{:S(2)}) copy-start(bf16[2,128,128]{2,1,0:T(8,128)(2,1)S(1)} %collective-permute-done.1) | copy-start | bytes 196612
  30.0 3.9 %collective-permute-start.2 = (bf16[2,128,128]{2,1,0:T(8,128)(2,1)}, bf16[2,128,128]{2,1,0:T(8,128)(2,1)}, u32[]{:S(2)}, u32[]{:S(2)}) collective-permute-start(bf16[2,128,128]{2,1,0:T(8,128)(2,1)} %fusion.26), channel_id=1, source_target_pairs={{0,16},{16,0},{4,20},{20,4},{8,24},{24,8},{12,28},{28,12},{1,17},{... | collective-permute-start | bytes 196616 | tf_op jit(solution)/shard_map/ppermute | solution.py:17
  31.1 6.1 %copy-start.6 = (bf16[6,64,2,128]{3,2,1,0:T(2,128)(2,1)S(1)}, bf16[6,64,2,128]{3,2,1,0:T(2,128)(2,1)}, u32[]{:S(2)}) copy-start(bf16[6,64,2,128]{3,2,1,0:T(2,128)(2,1)} %copy-done.4) | copy-start | bytes 589828
  31.1 6.9 %copy-start.15 = (bf16[6,2,64,64]{3,2,1,0:T(8,128)(2,1)S(1)}, bf16[6,2,64,64]{3,2,1,0:T(8,128)(2,1)}, u32[]{:S(2)}) copy-start(bf16[6,2,64,64]{3,2,1,0:T(8,128)(2,1)} %fusion.13) | copy-start | bytes 294916
  42.4 116.0 %reduce-scatter.3.cloned.1.call-start = ((), (), s32[]{:S(2)}) async-start(), calls=%async_computation.2 | async-start | bytes 3932160 | tf_op jit(solution)/shard_map/reduce_scatter | solution.py:85
  50.4 2.0 %copy-start.3 = (bf16[6,64,2,128]{3,2,1,0:T(2,128)(2,1)S(1)}, bf16[6,64,2,128]{3,2,1,0:T(2,128)(2,1)}, u32[]{:S(2)}) copy-start(bf16[6,64,2,128]{3,2,1,0:T(2,128)(2,1)} %copy-done.2) | copy-start | bytes 589828
  50.4 2.0 %copy-start.16 = (bf16[6,2,64,64]{3,2,1,0:T(8,128)(2,1)S(1)}, bf16[6,2,64,64]{3,2,1,0:T(8,128)(2,1)}, u32[]{:S(2)}) copy-start(bf16[6,2,64,64]{3,2,1,0:T(8,128)(2,1)} %fusion.13) | copy-start | bytes 294916
  52.0 2.1 %copy-start.7 = (bf16[6,64,2,128]{3,2,1,0:T(2,128)(2,1)S(1)}, bf16[6,64,2,128]{3,2,1,0:T(2,128)(2,1)}, u32[]{:S(2)}) copy-start(bf16[6,64,2,128]{3,2,1,0:T(2,128)(2,1)} %copy-done.4) | copy-start | bytes 589828
  52.0 2.1 %copy-start.17 = (bf16[6,2,64,64]{3,2,1,0:T(8,128)(2,1)S(1)}, bf16[6,2,64,64]{3,2,1,0:T(8,128)(2,1)}, u32[]{:S(2)}) copy-start(bf16[6,2,64,64]{3,2,1,0:T(8,128)(2,1)} %fusion.12) | copy-start | bytes 294916
  52.4 2.9 %copy-start.11 = (bf16[6,2,128,128]{3,2,1,0:T(8,128)(2,1)S(1)}, bf16[6,2,128,128]{3,2,1,0:T(8,128)(2,1)}, u32[]{:S(2)}) copy-start(bf16[6,2,128,128]{3,2,1,0:T(8,128)(2,1)} %copy-done.10) | copy-start | bytes 1179652
  52.9 2.8 %copy-start.9 = (bf16[6,2,128,128]{3,2,1,0:T(8,128)(2,1)S(1)}, bf16[6,2,128,128]{3,2,1,0:T(8,128)(2,1)}, u32[]{:S(2)}) copy-start(bf16[6,2,128,128]{3,2,1,0:T(8,128)(2,1)} %copy-done.8) | copy-start | bytes 1179652
  (5 other events, 4.7 us)
Sparse Core Ops, SparseCore 0:
  42.5 52.9 reduce-scatter.4
  98.4 59.8 reduce-scatter.2
where the time goes:
time: 168 us; the launch traced here: 165 us
  waiting for transfers between devices  102 us (61%)
  matrix products  19.3 us (11%)
  between operations  14.4 us (9%)
  local copies, waits for them, and re-layouts  14.3 us (9%)
  other arithmetic  11.2 us (7%)
  starting transfers between devices  3.89 us (2%)
    reduce_scatter x1, waiting for transfers between devices, local(): lax.psum_scatter(lax.dot_general(attention, out_weight, (((1,), (1,)), ((...  59 us
    reduce_scatter x1, waiting for transfers between devices, local(): lax.psum_scatter(lax.dot_general(out_grad, attention, (((0,), (0,)), ((),...  38.3 us
    unnamed x46, local copies, waits for them, and re-layouts  6.77 us
    ppermute x6, waiting for transfers between devices, swapped(): return lax.ppermute(block, axis, route)  4.89 us
    dot_general x1, matrix products, local(): lax.dot_general(attention, out_weight, (((1,), (1,)), ((), ())), preferre...  4.42 us
    ppermute x6, starting transfers between devices, swapped(): return lax.ppermute(block, axis, route)  3.81 us
  transfers between devices with their start and end apart: 8, of which 5 were waited for; matrix products, arithmetic and copies ran while one was open for 16% of the time, Pallas kernels for 0%

commit v1 on v0

--- a/solution.py
+++ b/solution.py
@@ -1,6 +1,10 @@
+import functools
+
 import jax
 import jax.numpy as jnp
 from jax import lax
+from jax.experimental import pallas as pl
+from jax.experimental.pallas import tpu as pltpu
 from jax.sharding import PartitionSpec as P
 
 HD = 128
@@ -123,9 +127,341 @@
     )
 
 
+def flipped(position, mask):
+    result = position
+    for bit in range(mask.bit_length()):
+        if mask >> bit & 1:
+            step = 1 << bit
+            result = result + (1 - 2 * (position // step % 2)) * step
+    return result
+
+
+def nn(a, b):
+    return jnp.dot(a, b, preferred_element_type=jnp.float32)
+
+
+def nt(a, b):
+    return lax.dot_general(a, b, (((1,), (1,)), ((), ())), preferred_element_type=jnp.float32)
+
+
+def tn(a, b):
+    return lax.dot_general(a, b, (((0,), (0,)), ((), ())), preferred_element_type=jnp.float32)
+
+
+def fused_kernel(
+    n_seq, n_head, q_ref, k_ref, v_ref, w_ref, og_ref,
+    out_ref, qg_ref, kg_ref, vg_ref, wg_ref,
+    wf, state_out, state_in, grad, att, att_t, att_in, acc,
+    part_out, part_in, sum_out, sum_in,
+    z_send, z_recv, p_send, p_recv, c_send, c_recv,
+    s_send, s_recv, a_send, a_recv, g_send, g_recv, r_send, r_recv,
+):
+    rows = q_ref.shape[0]
+    width = w_ref.shape[0]
+    heads = q_ref.shape[1] // HD
+    chips = n_seq // 2
+    block = width // n_seq
+    mine = rows // n_head
+    total_rows = rows * n_seq
+    factor = (HD * total_rows) ** (-0.5)
+    seq = lax.axis_index("seq")
+    z = lax.axis_index("head")
+    chip = seq // 2
+    core = seq % 2
+    partner = chip * 2 + 1 - core
+
+    def zpeer(dz):
+        return lax.rem(z + dz, n_head)
+
+    def peer_chip(k):
+        return flipped(chip, k)
+
+    def band(j):
+        return pl.ds(pl.multiple_of(j * block, block), block)
+
+    def remote(src, dst, send, recv, **where):
+        return pltpu.make_async_remote_copy(
+            src_ref=src, dst_ref=dst, send_sem=send, recv_sem=recv,
+            device_id=where, device_id_type=pl.DeviceIdType.MESH,
+        )
+
+    barrier = pltpu.get_barrier_semaphore()
+    for m in range(1, n_seq):
+        pl.semaphore_signal(
+            barrier, inc=1, device_id={"seq": flipped(seq, m)},
+            device_id_type=pl.DeviceIdType.MESH,
+        )
+    for dz in range(1, n_head):
+        pl.semaphore_signal(
+            barrier, inc=1, device_id={"head": zpeer(dz)},
+            device_id_type=pl.DeviceIdType.MESH,
+        )
+    pl.semaphore_wait(barrier, n_seq + n_head - 2)
+
+    def z_copy(dz):
+        back = n_head - dz
+        return remote(
+            w_ref.at[band(seq)], wf.at[back - 1, band(seq)],
+            z_send.at[dz - 1], z_recv.at[back - 1], head=zpeer(dz),
+        )
+
+    def z_wait(dz):
+        return remote(
+            w_ref.at[band(seq)], wf.at[dz - 1, band(seq)],
+            z_send.at[dz - 1], z_recv.at[dz - 1], head=zpeer(dz),
+        )
+
+    for dz in range(1, n_head):
+        z_copy(dz).start()
+
+    def state_copy(m, which):
+        return remote(
+            state_out.at[which], state_in.at[m - 1],
+            s_send.at[m - 1], s_recv.at[m - 1], seq=flipped(seq, m),
+        )
+
+    for h in range(heads):
+        cols = pl.ds(h * HD, HD)
+        state_out[0, h] = tn(k_ref[:, cols], v_ref[:, cols]).astype(jnp.bfloat16)
+    for m in range(1, n_seq):
+        @pl.when(flipped(seq, m) > seq)
+        def _():
+            state_copy(m, 0).start()
+
+    acc[0] = jnp.zeros(acc.shape[1:], jnp.float32)
+
+    @pl.loop(0, n_seq)
+    def _(j):
+        acc[0] += nn(og_ref[:, band(j)], w_ref[band(j), :])
+
+    grad[...] = acc[0].astype(jnp.bfloat16)
+    for h in range(heads):
+        cols = pl.ds(h * HD, HD)
+        state_out[1, h] = tn(q_ref[:, cols], grad[:, cols]).astype(jnp.bfloat16)
+    for m in range(1, n_seq):
+        @pl.when(flipped(seq, m) < seq)
+        def _():
+            state_copy(m, 1).start()
+
+    row = lax.broadcasted_iota(jnp.int32, (rows, rows), 0)
+    col = lax.broadcasted_iota(jnp.int32, (rows, rows), 1)
+    for h in range(heads):
+        cols = pl.ds(h * HD, HD)
+        q, k, v, g = q_ref[:, cols], k_ref[:, cols], v_ref[:, cols], grad[:, cols]
+        weights = jnp.where(row >= col, factor * nt(q, k), 0.0).astype(jnp.bfloat16)
+        acc[0, :, cols] = nn(weights, v)
+        weights = jnp.where(row >= col, factor * nt(g, v), 0.0).astype(jnp.bfloat16)
+        acc[1, :, cols] = nn(weights, k)
+        weights = jnp.where(row <= col, factor * nt(v, g), 0.0).astype(jnp.bfloat16)
+        acc[2, :, cols] = nn(weights, q)
+        weights = jnp.where(row <= col, factor * nt(k, q), 0.0).astype(jnp.bfloat16)
+        acc[3, :, cols] = nn(weights, g)
+
+    inflow = jnp.zeros(state_out.shape[1:], jnp.float32)
+    outflow = inflow
+    for m in range(1, n_seq):
+        state_copy(m, 0).wait_recv()
+        arrived = state_in[m - 1].astype(jnp.float32)
+        early = (flipped(seq, m) < seq).astype(jnp.float32)
+        inflow = inflow + early * arrived
+        outflow = outflow + (1.0 - early) * arrived
+    inflow = inflow.astype(jnp.bfloat16)
+    outflow = outflow.astype(jnp.bfloat16)
+    for h in range(heads):
+        cols = pl.ds(h * HD, HD)
+        full = acc[0, :, cols] + factor * nn(q_ref[:, cols], inflow[h])
+        att[:, cols] = full.astype(jnp.bfloat16)
+        att_t[cols, :] = full.T.astype(jnp.bfloat16)
+
+    def att_copy(dz):
+        back = n_head - dz
+        start = pl.multiple_of(zpeer(dz) * mine, mine)
+        return remote(
+            att.at[pl.ds(start, mine)], att_in.at[back - 1],
+            a_send.at[dz - 1], a_recv.at[back - 1], head=zpeer(dz),
+        )
+
+    for dz in range(1, n_head):
+        att_copy(dz).start()
+
+    def share(j):
+        return nn(att_t[...], og_ref[:, band(j)])
+
+    def part_copy(k):
+        return remote(
+            part_out.at[k], part_in.at[k], g_send.at[k], g_recv.at[k], seq=partner
+        )
+
+    def sum_copy(k):
+        return remote(
+            sum_out.at[k - 1], sum_in.at[k - 1], r_send.at[k - 1], r_recv.at[k - 1],
+            seq=peer_chip(k) * 2 + core,
+        )
+
+    order = list(range(1, chips))[::-1] + [0]
+    for k in order:
+        part_out[k] = share(peer_chip(k) * 2 + 1 - core).astype(jnp.bfloat16)
+        part_copy(k).start()
+
+    def p_copy(dz, k):
+        at = (dz - 1) * chips + k
+        return remote(
+            wf.at[dz - 1, band(seq)], wf.at[dz - 1, band(seq)],
+            p_send.at[at], p_recv.at[at], seq=peer_chip(k) * 2 + core,
+        )
+
+    def p_wait(dz, k):
+        at = (dz - 1) * chips + k
+        there = band(peer_chip(k) * 2 + core)
+        return remote(
+            wf.at[dz - 1, there], wf.at[dz - 1, there],
+            p_send.at[at], p_recv.at[at], seq=peer_chip(k) * 2 + core,
+        )
+
+    def c_copy(dz, k, side):
+        at = (dz - 1) * chips + k
+        there = band(peer_chip(k) * 2 + side)
+        return remote(
+            wf.at[dz - 1, there], wf.at[dz - 1, there],
+            c_send.at[at], c_recv.at[at], seq=partner,
+        )
+
+    hops = [1, 3, 2] if n_head == 4 else list(range(1, n_head))
+
+    def forward(dz):
+        z_wait(dz).wait_recv()
+        for k in range(chips - 1, 0, -1):
+            p_copy(dz, k).start()
+        c_copy(dz, 0, core).start()
+
+    forward(hops[0])
+    own = None
+    for k in order:
+        part_copy(k).wait_recv()
+        total = share(peer_chip(k) * 2 + core) + part_in[k].astype(jnp.float32)
+        if k:
+            sum_out[k - 1] = total.astype(jnp.bfloat16)
+            sum_copy(k).start()
+        else:
+            wg_ref[...] = total
+    for dz in hops[1:]:
+        forward(dz)
+
+    for h in range(heads):
+        cols = pl.ds(h * HD, HD)
+        q, k, v, g = q_ref[:, cols], k_ref[:, cols], v_ref[:, cols], grad[:, cols]
+        qg_ref[:, cols] = (acc[1, :, cols] + factor * nt(g, inflow[h])).astype(jnp.bfloat16)
+        kg_ref[:, cols] = (acc[2, :, cols] + factor * nt(v, outflow[h])).astype(jnp.bfloat16)
+        vg_ref[:, cols] = (acc[3, :, cols] + factor * nn(k, outflow[h])).astype(jnp.bfloat16)
+
+    for k in range(1, chips):
+        sum_copy(k).wait_recv()
+        wg_ref[...] += sum_in[k - 1].astype(jnp.float32)
+    wg_ref[...] = wg_ref[...] * total_rows ** (-0.5)
+
+    for dz in range(1, n_head):
+        att_copy(n_head - dz).wait_recv()
+
+    for dz in hops:
+        for k in range(1, chips):
+            p_wait(dz, k).wait_recv()
+            c_copy(dz, k, core).start()
+
+    at_home = pl.ds(pl.multiple_of(z * mine, mine), mine)
+
+    def finish(j):
+        there = band(j)
+        total = nt(att[at_home, :], w_ref[there, :]).astype(jnp.bfloat16).astype(jnp.float32)
+        for dz in range(1, n_head):
+            term = nt(att_in[dz - 1], wf[dz - 1, there, :])
+            total = total + term.astype(jnp.bfloat16).astype(jnp.float32)
+        out_ref[:, there] = total.astype(jnp.bfloat16)
+
+    @pl.loop(0, chips)
+    def _(p):
+        finish(p * 2 + core)
+
+    for dz in hops:
+        for k in range(chips):
+            c_copy(dz, k, 1 - core).wait_recv()
+
+    @pl.loop(0, chips)
+    def _(p):
+        finish(p * 2 + 1 - core)
+
+    for dz in range(1, n_head):
+        z_copy(dz).wait_send()
+        att_copy(dz).wait_send()
+        for k in range(chips):
+            if k:
+                p_copy(dz, k).wait_send()
+            c_copy(dz, k, core).wait_send()
+    for m in range(1, n_seq):
+        state_copy(m, 0).wait_send()
+    for k in range(chips):
+        part_copy(k).wait_send()
+        if k:
+            sum_copy(k).wait_send()
+
+
+def fused(n_seq, n_head, queries, key_rows, value_rows, out_weight, out_grad):
+    rows, inner = queries.shape
+    width = out_weight.shape[0]
+    heads = inner // HD
+    chips = n_seq // 2
+    block = width // n_seq
+    mine = rows // n_head
+    bf = jnp.bfloat16
+    vmem = pl.BlockSpec(memory_space=pltpu.VMEM)
+
+    def sems(count):
+        return pltpu.SemaphoreType.DMA((count,))
+
+    others = n_head - 1
+    output, query_grad, key_grad, value_grad, weight_grad = pl.pallas_call(
+        functools.partial(fused_kernel, n_seq, n_head),
+        out_shape=(
+            jax.ShapeDtypeStruct((mine, width), bf),
+            jax.ShapeDtypeStruct((rows, inner), bf),
+            jax.ShapeDtypeStruct((rows, inner), bf),
+            jax.ShapeDtypeStruct((rows, inner), bf),
+            jax.ShapeDtypeStruct((inner, block), jnp.float32),
+        ),
+        in_specs=[vmem] * 5,
+        out_specs=(vmem,) * 5,
+        scratch_shapes=[
+            pltpu.VMEM((others, width, inner), bf),
+            pltpu.VMEM((2, heads, HD, HD), bf),
+            pltpu.VMEM((n_seq - 1, heads, HD, HD), bf),
+            pltpu.VMEM((rows, inner), bf),
+            pltpu.VMEM((rows, inner), bf),
+            pltpu.VMEM((inner, rows), bf),
+            pltpu.VMEM((others, mine, inner), bf),
+            pltpu.VMEM((4, rows, inner), jnp.float32),
+            pltpu.VMEM((chips, inner, block), bf),
+            pltpu.VMEM((chips, inner, block), bf),
+            pltpu.VMEM((chips - 1, inner, block), bf),
+            pltpu.VMEM((chips - 1, inner, block), bf),
+            sems(others), sems(others),
+            sems(others * chips), sems(others * chips),
+            sems(others * chips), sems(others * chips),
+            sems(n_seq - 1), sems(n_seq - 1),
+            sems(others), sems(others),
+            sems(chips), sems(chips),
+            sems(chips - 1), sems(chips - 1),
+        ],
+        compiler_params=pltpu.CompilerParams(
+            collective_id=0, has_side_effects=True, vmem_limit_bytes=44 << 20
+        ),
+    )(queries, key_rows, value_rows, out_weight, out_grad)
+    return output, query_grad, key_grad, value_grad, weight_grad.T
+
+
 def solution(mesh):
+    sizes = (mesh.shape["seq"], mesh.shape["head"])
+    body = functools.partial(fused, *sizes) if sizes == (8, 4) else local
     return jax.shard_map(
-        local,
+        body,
         mesh=mesh,
         in_specs=(
             P("seq", "head"),

time: 168 us -> 92 us (0.55); the launches traced: 165 us -> 91.7 us
  waiting for transfers between devices: 102 us -> 0 us
  Pallas kernels: 0 us -> 80.9 us
  matrix products: 19.3 us -> 0 us
  between operations: 14.4 us -> 0.66 us
  other arithmetic: 11.2 us -> 0 us
  local copies, waits for them, and re-layouts: 14.3 us -> 10.2 us
  starting transfers between devices: 3.89 us -> 0 us
    reduce_scatter x2 -> x0, waiting for transfers between devices: 97.3 us -> none  [the longest x1 59 us: local(): lax.psum_scatter(lax.dot_general(attention, out_weight, (((1,), (1,)), ((...]
    pallas_call x0 -> x1, Pallas kernels: none -> 80.9 us  [fused(): pl.pallas_call(functools.partial(fused_kernel, n_seq, n_head), out_shape=...]
    dot_general x19 -> x0, matrix products: 19.3 us -> none  [the longest x1 4.42 us: local(): lax.dot_general(attention, out_weight, (((1,), (1,)), ((), ())), preferre...]
    convert_element_type x7 -> x0, other arithmetic: 5.28 us -> none  [the longest x3 3.02 us: local(): pairs_total.astype(jnp.bfloat16)]
    ppermute x6 -> x0, waiting for transfers between devices: 4.89 us -> none  [swapped(): return lax.ppermute(block, axis, route)]
    reshape x4 -> x0, local copies, waits for them, and re-layouts: 4.06 us -> none  [the longest x1 1.13 us: local(): query_blocks = queries.reshape(block_shape)]
    ppermute x6 -> x0, starting transfers between devices: 3.81 us -> none  [swapped(): return lax.ppermute(block, axis, route)]
    unnamed x46 -> x15, local copies, waits for them, and re-layouts: 6.77 us -> 10.2 us
  transfers between devices with their start and end apart: 8 -> 0, of which waited for: 5 -> 0; matrix products, arithmetic and copies ran while one was open for 16% -> 0% of each run, Pallas kernels for 0% -> 0%
where the time goes in v1:
time: 92 us; the launch traced here: 91.7 us
  Pallas kernels  80.9 us (88%)
  local copies, waits for them, and re-layouts  10.2 us (11%)
    pallas_call x1, Pallas kernels, fused(): pl.pallas_call(functools.partial(fused_kernel, n_seq, n_head), out_shape=...  80.9 us
    unnamed x15, local copies, waits for them, and re-layouts  10.2 us

profile of v1, /device:TPU:11, one launch (start us, length us, event | category | flops | bytes accessed | tf_op | source)
XLA Modules:
  0.0 91.7 jit_solution(5087857949996127033)
XLA Ops:
  0.6 0.0 copy-start
  0.6 1.9 %copy-done = bf16[384,4096]{1,0:T(8,128)(2,1)S(1)} copy-done((bf16[384,4096]{1,0:T(8,128)(2,1)S(1)}, bf16[384,4096]{1,0:T(8,128)(2,1)}, u32[]{:S(2)}) %copy-start) | copy-done | bytes 3145752
  2.5 0.0 copy-start.1
  2.5 1.6 %copy-done.1 = bf16[4096,256]{1,0:T(8,128)(2,1)S(1)} copy-done((bf16[4096,256]{1,0:T(8,128)(2,1)S(1)}, bf16[4096,256]{1,0:T(8,128)(2,1)}, u32[]{:S(2)}) %copy-start.1) | copy-done | bytes 2097176
  4.1 0.0 copy-start.2
  4.1 0.9 %copy-done.2 = bf16[384,256]{1,0:T(8,128)(2,1)S(1)} copy-done((bf16[384,256]{1,0:T(8,128)(2,1)S(1)}, bf16[384,256]{1,0:T(8,128)(2,1)}, u32[]{:S(2)}) %copy-start.2) | copy-done | bytes 196632
  5.0 0.0 copy-start.3
  5.0 0.9 %copy-done.3 = bf16[384,256]{1,0:T(8,128)(2,1)S(1)} copy-done((bf16[384,256]{1,0:T(8,128)(2,1)S(1)}, bf16[384,256]{1,0:T(8,128)(2,1)}, u32[]{:S(2)}) %copy-start.3) | copy-done | bytes 196632
  6.0 0.0 copy-start.4
  6.0 0.9 %copy-done.4 = bf16[384,256]{1,0:T(8,128)(2,1)S(1)} copy-done((bf16[384,256]{1,0:T(8,128)(2,1)S(1)}, bf16[384,256]{1,0:T(8,128)(2,1)}, u32[]{:S(2)}) %copy-start.4) | copy-done | bytes 196632
  6.9 80.9 %shard_map.92 = (bf16[96,4096]{1,0:T(8,128)(2,1)S(1)}, bf16[384,256]{1,0:T(8,128)(2,1)S(1)}, bf16[384,256]{1,0:T(8,128)(2,1)S(1)}, bf16[384,256]{1,0:T(8,128)(2,1)S(1)}, f32[256,512]{1,0:T(8,128)S(1)}) custom-call(bf16[384,256]{1,0:T(8,128)(2,1)S(1)} %copy-done.2, bf16[384,256]{1,0:T(8,128)(2,1)S(1)} %copy-done.3, bf16[384,256]{1,0:T(8,128)(2,1)S(1)} %copy-done.4, ...), custom_call_target="tpu_custom_call" | custom-call | tf_op jit(solution)/shard_map/pallas_call | solution.py:421
  87.8 1.0 %copy.10 = f32[512,256]{1,0:T(8,128)} copy(f32[512,256]{0,1:T(8,128)S(1)} %bitcast.1) | data formatting | bytes 1048576
  88.8 0.9 copy.15
  89.7 0.7 copy.16
  90.4 0.7 copy.17
  91.0 0.7 copy.18
Async XLA Ops:
  0.6 1.9 %copy-start = (bf16[384,4096]{1,0:T(8,128)(2,1)S(1)}, bf16[384,4096]{1,0:T(8,128)(2,1)}, u32[]{:S(2)}) copy-start(bf16[384,4096]{1,0:T(8,128)(2,1)} %og_ref.1) | copy-start | bytes 9437188
  2.5 1.6 %copy-start.1 = (bf16[4096,256]{1,0:T(8,128)(2,1)S(1)}, bf16[4096,256]{1,0:T(8,128)(2,1)}, u32[]{:S(2)}) copy-start(bf16[4096,256]{1,0:T(8,128)(2,1)} %w_ref.1) | copy-start | bytes 6291460
  4.1 0.9 %copy-start.2 = (bf16[384,256]{1,0:T(8,128)(2,1)S(1)}, bf16[384,256]{1,0:T(8,128)(2,1)}, u32[]{:S(2)}) copy-start(bf16[384,256]{1,0:T(8,128)(2,1)} %q_ref.1) | copy-start | bytes 589828
  5.0 0.9 %copy-start.3 = (bf16[384,256]{1,0:T(8,128)(2,1)S(1)}, bf16[384,256]{1,0:T(8,128)(2,1)}, u32[]{:S(2)}) copy-start(bf16[384,256]{1,0:T(8,128)(2,1)} %k_ref.1) | copy-start | bytes 589828
  6.0 0.9 %copy-start.4 = (bf16[384,256]{1,0:T(8,128)(2,1)S(1)}, bf16[384,256]{1,0:T(8,128)(2,1)}, u32[]{:S(2)}) copy-start(bf16[384,256]{1,0:T(8,128)(2,1)} %v_ref.1) | copy-start | bytes 589828

commit v2 on v1

--- a/solution.py
+++ b/solution.py
@@ -149,9 +149,11 @@
 
 
 def fused_kernel(
-    n_seq, n_head, q_ref, k_ref, v_ref, w_ref, og_ref,
-    out_ref, qg_ref, kg_ref, vg_ref, wg_ref,
-    wf, state_out, state_in, grad, att, att_t, att_in, acc,
+    n_seq, n_head, q_hbm, k_hbm, v_hbm, w_hbm, og_hbm,
+    out_hbm, qg_hbm, kg_hbm, vg_hbm, wg_hbm,
+    out_ref, qg_ref, kg_ref, vg_ref, wg_ref, out_sem,
+    q_ref, k_ref, v_ref, w_ref, og_ref, in_sem,
+    wf, state_out, state_in, grad, att, att_t, att_in, acc, gathered, out_acc,
     part_out, part_in, sum_out, sum_in,
     z_send, z_recv, p_send, p_recv, c_send, c_recv,
     s_send, s_recv, a_send, a_recv, g_send, g_recv, r_send, r_recv,
@@ -185,6 +187,14 @@
             device_id=where, device_id_type=pl.DeviceIdType.MESH,
         )
 
+    loads = [
+        pltpu.make_async_copy(there, here, in_sem.at[at])
+        for at, (there, here) in enumerate((
+            (k_hbm, k_ref), (v_hbm, v_ref), (og_hbm, og_ref), (w_hbm, w_ref), (q_hbm, q_ref)
+        ))
+    ]
+    for load in loads:
+        load.start()
     barrier = pltpu.get_barrier_semaphore()
     for m in range(1, n_seq):
         pl.semaphore_signal(
@@ -201,13 +211,13 @@
     def z_copy(dz):
         back = n_head - dz
         return remote(
-            w_ref.at[band(seq)], wf.at[back - 1, band(seq)],
+            w_hbm.at[band(seq)], wf.at[back - 1, band(seq)],
             z_send.at[dz - 1], z_recv.at[back - 1], head=zpeer(dz),
         )
 
     def z_wait(dz):
         return remote(
-            w_ref.at[band(seq)], wf.at[dz - 1, band(seq)],
+            w_hbm.at[band(seq)], wf.at[dz - 1, band(seq)],
             z_send.at[dz - 1], z_recv.at[dz - 1], head=zpeer(dz),
         )
 
@@ -220,6 +230,8 @@
             s_send.at[m - 1], s_recv.at[m - 1], seq=flipped(seq, m),
         )
 
+    loads[0].wait()
+    loads[1].wait()
     for h in range(heads):
         cols = pl.ds(h * HD, HD)
         state_out[0, h] = tn(k_ref[:, cols], v_ref[:, cols]).astype(jnp.bfloat16)
@@ -229,12 +241,15 @@
             state_copy(m, 0).start()
 
     acc[0] = jnp.zeros(acc.shape[1:], jnp.float32)
+    loads[2].wait()
+    loads[3].wait()
 
     @pl.loop(0, n_seq)
     def _(j):
         acc[0] += nn(og_ref[:, band(j)], w_ref[band(j), :])
 
     grad[...] = acc[0].astype(jnp.bfloat16)
+    loads[4].wait()
     for h in range(heads):
         cols = pl.ds(h * HD, HD)
         state_out[1, h] = tn(q_ref[:, cols], grad[:, cols]).astype(jnp.bfloat16)
@@ -257,6 +272,38 @@
         weights = jnp.where(row <= col, factor * nt(k, q), 0.0).astype(jnp.bfloat16)
         acc[3, :, cols] = nn(weights, g)
 
+    def p_copy(dz, k):
+        at = (dz - 1) * chips + k
+        return remote(
+            wf.at[dz - 1, band(seq)], wf.at[dz - 1, band(seq)],
+            p_send.at[at], p_recv.at[at], seq=peer_chip(k) * 2 + core,
+        )
+
+    def p_wait(dz, k):
+        at = (dz - 1) * chips + k
+        there = band(peer_chip(k) * 2 + core)
+        return remote(
+            wf.at[dz - 1, there], wf.at[dz - 1, there],
+            p_send.at[at], p_recv.at[at], seq=peer_chip(k) * 2 + core,
+        )
+
+    def c_copy(dz, k, side):
+        at = (dz - 1) * chips + k
+        there = band(peer_chip(k) * 2 + side)
+        return remote(
+            wf.at[dz - 1, there], wf.at[dz - 1, there],
+            c_send.at[at], c_recv.at[at], seq=partner,
+        )
+
+    hops = [1, 3, 2] if n_head == 4 else list(range(1, n_head))
+
+    def forward(dz):
+        z_wait(dz).wait_recv()
+        for k in range(chips - 1, 0, -1):
+            p_copy(dz, k).start()
+        c_copy(dz, 0, core).start()
+
+    forward(hops[0])
     inflow = jnp.zeros(state_out.shape[1:], jnp.float32)
     outflow = inflow
     for m in range(1, n_seq):
@@ -303,39 +350,7 @@
         part_out[k] = share(peer_chip(k) * 2 + 1 - core).astype(jnp.bfloat16)
         part_copy(k).start()
 
-    def p_copy(dz, k):
-        at = (dz - 1) * chips + k
-        return remote(
-            wf.at[dz - 1, band(seq)], wf.at[dz - 1, band(seq)],
-            p_send.at[at], p_recv.at[at], seq=peer_chip(k) * 2 + core,
-        )
-
-    def p_wait(dz, k):
-        at = (dz - 1) * chips + k
-        there = band(peer_chip(k) * 2 + core)
-        return remote(
-            wf.at[dz - 1, there], wf.at[dz - 1, there],
-            p_send.at[at], p_recv.at[at], seq=peer_chip(k) * 2 + core,
-        )
-
-    def c_copy(dz, k, side):
-        at = (dz - 1) * chips + k
-        there = band(peer_chip(k) * 2 + side)
-        return remote(
-            wf.at[dz - 1, there], wf.at[dz - 1, there],
-            c_send.at[at], c_recv.at[at], seq=partner,
-        )
-
-    hops = [1, 3, 2] if n_head == 4 else list(range(1, n_head))
-
-    def forward(dz):
-        z_wait(dz).wait_recv()
-        for k in range(chips - 1, 0, -1):
-            p_copy(dz, k).start()
-        c_copy(dz, 0, core).start()
-
-    forward(hops[0])
-    own = None
+    forward(hops[1])
     for k in order:
         part_copy(k).wait_recv()
         total = share(peer_chip(k) * 2 + core) + part_in[k].astype(jnp.float32)
@@ -343,8 +358,8 @@
             sum_out[k - 1] = total.astype(jnp.bfloat16)
             sum_copy(k).start()
         else:
-            wg_ref[...] = total
-    for dz in hops[1:]:
+            gathered[...] = total
+    for dz in hops[2:]:
         forward(dz)
 
     for h in range(heads):
@@ -354,41 +369,54 @@
         kg_ref[:, cols] = (acc[2, :, cols] + factor * nt(v, outflow[h])).astype(jnp.bfloat16)
         vg_ref[:, cols] = (acc[3, :, cols] + factor * nn(k, outflow[h])).astype(jnp.bfloat16)
 
-    for k in range(1, chips):
-        sum_copy(k).wait_recv()
-        wg_ref[...] += sum_in[k - 1].astype(jnp.float32)
-    wg_ref[...] = wg_ref[...] * total_rows ** (-0.5)
-
+    stores = [
+        pltpu.make_async_copy(here, there, out_sem.at[at])
+        for at, (here, there) in enumerate((
+            (qg_ref, qg_hbm), (kg_ref, kg_hbm), (vg_ref, vg_hbm),
+            (wg_ref, wg_hbm), (out_ref, out_hbm),
+        ))
+    ]
+    for store in stores[:3]:
+        store.start()
     for dz in range(1, n_head):
         att_copy(n_head - dz).wait_recv()
 
-    for dz in hops:
+    at_home = pl.ds(pl.multiple_of(z * mine, mine), mine)
+
+    @pl.loop(0, n_seq)
+    def _(j):
+        there = band(j)
+        own = nt(att[at_home, :], w_ref[there, :])
+        out_acc[:, there] = own.astype(jnp.bfloat16).astype(jnp.float32)
+
+    def add(dz, side):
+        @pl.loop(0, chips)
+        def _(p):
+            there = band(p * 2 + side)
+            term = nt(att_in[dz - 1], wf[dz - 1, there, :])
+            out_acc[:, there] += term.astype(jnp.bfloat16).astype(jnp.float32)
+
+    def add_other(dz):
+        for k in range(chips):
+            c_copy(dz, k, 1 - core).wait_recv()
+        add(dz, 1 - core)
+
+    for at, dz in enumerate(hops):
         for k in range(1, chips):
             p_wait(dz, k).wait_recv()
             c_copy(dz, k, core).start()
-
-    at_home = pl.ds(pl.multiple_of(z * mine, mine), mine)
-
-    def finish(j):
-        there = band(j)
-        total = nt(att[at_home, :], w_ref[there, :]).astype(jnp.bfloat16).astype(jnp.float32)
-        for dz in range(1, n_head):
-            term = nt(att_in[dz - 1], wf[dz - 1, there, :])
-            total = total + term.astype(jnp.bfloat16).astype(jnp.float32)
-        out_ref[:, there] = total.astype(jnp.bfloat16)
-
-    @pl.loop(0, chips)
-    def _(p):
-        finish(p * 2 + core)
-
-    for dz in hops:
-        for k in range(chips):
-            c_copy(dz, k, 1 - core).wait_recv()
-
-    @pl.loop(0, chips)
-    def _(p):
-        finish(p * 2 + 1 - core)
-
+        add(dz, core)
+        if at:
+            add_other(hops[at - 1])
+    for k in range(1, chips):
+        sum_copy(k).wait_recv()
+        gathered[...] += sum_in[k - 1].astype(jnp.float32)
+    wg_ref[...] = (gathered[...] * total_rows ** (-0.5)).T
+    stores[3].start()
+
+    add_other(hops[-1])
+    out_ref[...] = out_acc[...].astype(jnp.bfloat16)
+    stores[4].start()
     for dz in range(1, n_head):
         z_copy(dz).wait_send()
         att_copy(dz).wait_send()
@@ -402,6 +430,19 @@
         part_copy(k).wait_send()
         if k:
             sum_copy(k).wait_send()
+    for store in stores:
+        store.wait()
+
+
+def hand_over(*refs):
+    sem = refs[-1]
+    copies = [
+        pltpu.make_async_copy(refs[at], refs[at + 5], sem.at[at]) for at in range(5)
+    ]
+    for copy in copies:
+        copy.start()
+    for copy in copies:
+        copy.wait()
 
 
 def fused(n_seq, n_head, queries, key_rows, value_rows, out_weight, out_grad):
@@ -412,24 +453,36 @@
     block = width // n_seq
     mine = rows // n_head
     bf = jnp.bfloat16
-    vmem = pl.BlockSpec(memory_space=pltpu.VMEM)
+    hbm = pl.BlockSpec(memory_space=pltpu.HBM)
 
     def sems(count):
         return pltpu.SemaphoreType.DMA((count,))
 
     others = n_head - 1
-    output, query_grad, key_grad, value_grad, weight_grad = pl.pallas_call(
+    results = pl.pallas_call(
         functools.partial(fused_kernel, n_seq, n_head),
         out_shape=(
             jax.ShapeDtypeStruct((mine, width), bf),
             jax.ShapeDtypeStruct((rows, inner), bf),
             jax.ShapeDtypeStruct((rows, inner), bf),
             jax.ShapeDtypeStruct((rows, inner), bf),
-            jax.ShapeDtypeStruct((inner, block), jnp.float32),
+            jax.ShapeDtypeStruct((block, inner), jnp.float32),
         ),
-        in_specs=[vmem] * 5,
-        out_specs=(vmem,) * 5,
+        in_specs=[hbm] * 5,
+        out_specs=(hbm,) * 5,
         scratch_shapes=[
+            pltpu.VMEM((mine, width), bf),
+            pltpu.VMEM((rows, inner), bf),
+            pltpu.VMEM((rows, inner), bf),
+            pltpu.VMEM((rows, inner), bf),
+            pltpu.VMEM((block, inner), jnp.float32),
+            sems(5),
+            pltpu.VMEM((rows, inner), bf),
+            pltpu.VMEM((rows, inner), bf),
+            pltpu.VMEM((rows, inner), bf),
+            pltpu.VMEM((width, inner), bf),
+            pltpu.VMEM((rows, width), bf),
+            sems(5),
             pltpu.VMEM((others, width, inner), bf),
             pltpu.VMEM((2, heads, HD, HD), bf),
             pltpu.VMEM((n_seq - 1, heads, HD, HD), bf),
@@ -438,6 +491,8 @@
             pltpu.VMEM((inner, rows), bf),
             pltpu.VMEM((others, mine, inner), bf),
             pltpu.VMEM((4, rows, inner), jnp.float32),
+            pltpu.VMEM((inner, block), jnp.float32),
+            pltpu.VMEM((mine, width), jnp.float32),
             pltpu.VMEM((chips, inner, block), bf),
             pltpu.VMEM((chips, inner, block), bf),
             pltpu.VMEM((chips - 1, inner, block), bf),
@@ -451,10 +506,17 @@
             sems(chips - 1), sems(chips - 1),
         ],
         compiler_params=pltpu.CompilerParams(
-            collective_id=0, has_side_effects=True, vmem_limit_bytes=44 << 20
+            collective_id=0, has_side_effects=True, vmem_limit_bytes=62 << 20
         ),
     )(queries, key_rows, value_rows, out_weight, out_grad)
-    return output, query_grad, key_grad, value_grad, weight_grad.T
+    return pl.pallas_call(
+        hand_over,
+        out_shape=tuple(jax.ShapeDtypeStruct(r.shape, r.dtype) for r in results),
+        in_specs=[hbm] * 5,
+        out_specs=(hbm,) * 5,
+        scratch_shapes=[sems(5)],
+        compiler_params=pltpu.CompilerParams(vmem_limit_bytes=62 << 20),
+    )(*results)
 
 
 def solution(mesh):

time: 92 us -> 141 us (1.53)
  Pallas kernels: 80.9 us -> 140 us
  local copies, waits for them, and re-layouts: 10.2 us -> 0 us
    pallas_call x0 -> x1, Pallas kernels: none -> 58.7 us  [fused(): pl.pallas_call(hand_over, out_shape=tuple((jax.ShapeDtypeStruct(r.shape,...]
    unnamed x15 -> x0, local copies, waits for them, and re-layouts: 10.2 us -> none
where the time goes in v2:
time: 141 us
  Pallas kernels  140 us (99%)
    pallas_call x1, Pallas kernels, fused(): pl.pallas_call(functools.partial(fused_kernel, n_seq, n_head), out_shape=...  81.3 us
    pallas_call x1, Pallas kernels, fused(): pl.pallas_call(hand_over, out_shape=tuple((jax.ShapeDtypeStruct(r.shape,...  58.7 us

profile of v2, /device:TPU:11, one launch (start us, length us, event | category | flops | bytes accessed | tf_op | source)
XLA Modules:
  0.0 140.7 jit_solution(6161606692848170017)
XLA Ops:
  0.6 81.3 %shard_map.92 = (bf16[96,4096]{1,0:T(8,128)(2,1)}, bf16[384,256]{1,0:T(8,128)(2,1)}, bf16[384,256]{1,0:T(8,128)(2,1)}, bf16[384,256]{1,0:T(8,128)(2,1)}, f32[512,256]{1,0:T(8,128)}) custom-call(bf16[384,256]{1,0:T(8,128)(2,1)} %q_hbm.1, bf16[384,256]{1,0:T(8,128)(2,1)} %k_hbm.1, bf16[384,256]{1,0:T(8,128)(2,1)} %v_hbm.1, bf16[4096,256]{1,0:T(8,128)(2,1)} %w_hbm.1, ...), custom_call_target="tpu_custom_call" | custom-call | tf_op jit(solution)/shard_map/pallas_call | solution.py:462
  81.9 58.7 %shard_map.93 = (bf16[96,4096]{1,0:T(8,128)(2,1)}, bf16[384,256]{1,0:T(8,128)(2,1)}, bf16[384,256]{1,0:T(8,128)(2,1)}, bf16[384,256]{1,0:T(8,128)(2,1)}, f32[512,256]{1,0:T(8,128)}) custom-call(bf16[96,4096]{1,0:T(8,128)(2,1)} %get-tuple-element.10.refs_0_, bf16[384,256]{1,0:T(8,128)(2,1)} %get-tuple-element.11.refs_1_, ...), custom_call_target="tpu_custom_call" | custom-call | tf_op jit(solution)/shard_map/pallas_call | solution.py:512

commit v3 on v2

--- a/solution.py
+++ b/solution.py
@@ -435,14 +435,20 @@
 
 
 def hand_over(*refs):
-    sem = refs[-1]
-    copies = [
-        pltpu.make_async_copy(refs[at], refs[at + 5], sem.at[at]) for at in range(5)
+    sources, targets, held, sem = refs[:5], refs[5:10], refs[10:15], refs[15]
+    loads = [
+        pltpu.make_async_copy(sources[at], held[at], sem.at[at]) for at in range(5)
     ]
-    for copy in copies:
-        copy.start()
-    for copy in copies:
-        copy.wait()
+    stores = [
+        pltpu.make_async_copy(held[at], targets[at], sem.at[at + 5]) for at in range(5)
+    ]
+    for load in loads:
+        load.start()
+    for load, store in zip(loads, stores):
+        load.wait()
+        store.start()
+    for store in stores:
+        store.wait()
 
 
 def fused(n_seq, n_head, queries, key_rows, value_rows, out_weight, out_grad):
@@ -514,7 +520,7 @@
         out_shape=tuple(jax.ShapeDtypeStruct(r.shape, r.dtype) for r in results),
         in_specs=[hbm] * 5,
         out_specs=(hbm,) * 5,
-        scratch_shapes=[sems(5)],
+        scratch_shapes=[pltpu.VMEM(r.shape, r.dtype) for r in results] + [sems(10)],
         compiler_params=pltpu.CompilerParams(vmem_limit_bytes=62 << 20),
     )(*results)
 

time: 141 us -> 84.5 us (0.60)
  Pallas kernels: 140 us -> 83.8 us
    pallas_call x1, Pallas kernels: 58.7 us -> 2.47 us  [fused(): pl.pallas_call(hand_over, out_shape=tuple((jax.ShapeDtypeStruct(r.shape,...]
where the time goes in v3:
time: 84.5 us; the launch traced here: 84.4 us
  Pallas kernels  83.8 us (99%)
    pallas_call x1, Pallas kernels, fused(): pl.pallas_call(functools.partial(fused_kernel, n_seq, n_head), out_shape=...  81.3 us
    pallas_call x1, Pallas kernels, fused(): pl.pallas_call(hand_over, out_shape=tuple((jax.ShapeDtypeStruct(r.shape,...  2.47 us

profile of v3, /device:TPU:11, one launch (start us, length us, event | category | flops | bytes accessed | tf_op | source)
XLA Modules:
  0.0 84.4 jit_solution(8135063559192116183)
XLA Ops:
  0.6 81.3 %shard_map.92 = (bf16[96,4096]{1,0:T(8,128)(2,1)}, bf16[384,256]{1,0:T(8,128)(2,1)}, bf16[384,256]{1,0:T(8,128)(2,1)}, bf16[384,256]{1,0:T(8,128)(2,1)}, f32[512,256]{1,0:T(8,128)}) custom-call(bf16[384,256]{1,0:T(8,128)(2,1)} %q_hbm.1, bf16[384,256]{1,0:T(8,128)(2,1)} %k_hbm.1, bf16[384,256]{1,0:T(8,128)(2,1)} %v_hbm.1, bf16[4096,256]{1,0:T(8,128)(2,1)} %w_hbm.1, ...), custom_call_target="tpu_custom_call" | custom-call | tf_op jit(solution)/shard_map/pallas_call | solution.py:468
  81.9 2.5 %shard_map.93 = (bf16[96,4096]{1,0:T(8,128)(2,1)}, bf16[384,256]{1,0:T(8,128)(2,1)}, bf16[384,256]{1,0:T(8,128)(2,1)}, bf16[384,256]{1,0:T(8,128)(2,1)}, f32[512,256]{1,0:T(8,128)}) custom-call(bf16[96,4096]{1,0:T(8,128)(2,1)} %get-tuple-element.10.refs_0_, bf16[384,256]{1,0:T(8,128)(2,1)} %get-tuple-element.11.refs_1_, ...), custom_call_target="tpu_custom_call" | custom-call | tf_op jit(solution)/shard_map/pallas_call | solution.py:518

commit v4 on v3

--- a/solution.py
+++ b/solution.py
@@ -299,9 +299,27 @@
 
     def forward(dz):
         z_wait(dz).wait_recv()
-        for k in range(chips - 1, 0, -1):
+        for k in (2, 1):
             p_copy(dz, k).start()
         c_copy(dz, 0, core).start()
+
+    def half_copy(dz, k, source, target):
+        at = (dz - 1) * chips + k
+        size = block // 2
+        start = (peer_chip(source) * 2 + core) * block + (0 if k else size)
+        there = pl.ds(pl.multiple_of(start, size), size)
+        return remote(
+            wf.at[dz - 1, there], wf.at[dz - 1, there],
+            p_send.at[at], p_recv.at[at], seq=peer_chip(target) * 2 + core,
+        )
+
+    def relay(dz):
+        p_wait(dz, 1).wait_recv()
+        half_copy(dz, 3, 1, 2).start()
+        c_copy(dz, 1, core).start()
+        p_wait(dz, 2).wait_recv()
+        half_copy(dz, 0, 2, 1).start()
+        c_copy(dz, 2, core).start()
 
     forward(hops[0])
     inflow = jnp.zeros(state_out.shape[1:], jnp.float32)
@@ -361,6 +379,7 @@
             gathered[...] = total
     for dz in hops[2:]:
         forward(dz)
+    relay(hops[0])
 
     for h in range(heads):
         cols = pl.ds(h * HD, HD)
@@ -378,6 +397,7 @@
     ]
     for store in stores[:3]:
         store.start()
+    relay(hops[1])
     for dz in range(1, n_head):
         att_copy(n_head - dz).wait_recv()
 
@@ -401,10 +421,12 @@
             c_copy(dz, k, 1 - core).wait_recv()
         add(dz, 1 - core)
 
+    for dz in hops[2:]:
+        relay(dz)
     for at, dz in enumerate(hops):
-        for k in range(1, chips):
-            p_wait(dz, k).wait_recv()
-            c_copy(dz, k, core).start()
+        half_copy(dz, 3, 3, 2).wait_recv()
+        half_copy(dz, 0, 3, 1).wait_recv()
+        c_copy(dz, 3, core).start()
         add(dz, core)
         if at:
             add_other(hops[at - 1])
@@ -421,8 +443,10 @@
         z_copy(dz).wait_send()
         att_copy(dz).wait_send()
         for k in range(chips):
-            if k:
+            if k in (1, 2):
                 p_copy(dz, k).wait_send()
+            else:
+                half_copy(dz, k, 1 if k else 2, 2 if k else 1).wait_send()
             c_copy(dz, k, core).wait_send()
     for m in range(1, n_seq):
         state_copy(m, 0).wait_send()

time: 84.5 us -> 76 us (0.90)
  Pallas kernels: 83.8 us -> 74.8 us
    pallas_call x1, Pallas kernels: 81.3 us -> 72.3 us  [fused(): pl.pallas_call(functools.partial(fused_kernel, n_seq, n_head), out_shape=...]
where the time goes in v4:
time: 76 us; the launch traced here: 75.4 us
  Pallas kernels  74.8 us (98%)
    pallas_call x1, Pallas kernels, fused(): pl.pallas_call(functools.partial(fused_kernel, n_seq, n_head), out_shape=...  72.3 us
    pallas_call x1, Pallas kernels, fused(): pl.pallas_call(hand_over, out_shape=tuple((jax.ShapeDtypeStruct(r.shape,...  2.47 us

profile of v4, /device:TPU:11, one launch (start us, length us, event | category | flops | bytes accessed | tf_op | source)
XLA Modules:
  0.0 75.4 jit_solution(595260656614644938)
XLA Ops:
  0.6 72.3 %shard_map.92 = (bf16[96,4096]{1,0:T(8,128)(2,1)}, bf16[384,256]{1,0:T(8,128)(2,1)}, bf16[384,256]{1,0:T(8,128)(2,1)}, bf16[384,256]{1,0:T(8,128)(2,1)}, f32[512,256]{1,0:T(8,128)}) custom-call(bf16[384,256]{1,0:T(8,128)(2,1)} %q_hbm.1, bf16[384,256]{1,0:T(8,128)(2,1)} %k_hbm.1, bf16[384,256]{1,0:T(8,128)(2,1)} %v_hbm.1, bf16[4096,256]{1,0:T(8,128)(2,1)} %w_hbm.1, ...), custom_call_target="tpu_custom_call" | custom-call | tf_op jit(solution)/shard_map/pallas_call | solution.py:492
  73.0 2.5 %shard_map.93 = (bf16[96,4096]{1,0:T(8,128)(2,1)}, bf16[384,256]{1,0:T(8,128)(2,1)}, bf16[384,256]{1,0:T(8,128)(2,1)}, bf16[384,256]{1,0:T(8,128)(2,1)}, f32[512,256]{1,0:T(8,128)}) custom-call(bf16[96,4096]{1,0:T(8,128)(2,1)} %get-tuple-element.10.refs_0_, bf16[384,256]{1,0:T(8,128)(2,1)} %get-tuple-element.11.refs_1_, ...), custom_call_target="tpu_custom_call" | custom-call | tf_op jit(solution)/shard_map/pallas_call | solution.py:542
